TPU v7x, 256 devices: a whole 4x4x8 slice. The times are simulated.
256 devices in a mesh: dp: 8 (over z), nbr: 16 (over x_hi, y, core), mp: 2 (over x_lo).
Axes of the slice: x: 4 (x_hi: 2, x_lo: 2; x = x_hi * 2 + x_lo), y: 4, z: 8, core: 2. Of those that a mesh axis runs over, the one named last changes fastest.
Arguments:
- dec_rows: bfloat16 [8, 4096, 4096], P('dp', 'nbr'), may hold values from -6 to 6
- owner_shift: int32 [8, 4, 2], P('dp'), may hold values from 0 to 15, as said below
- nbr_rows: bfloat16 [8, 128, 128, 1024], P('dp', 'nbr', 'mp'), may hold values from -6 to 6
- cot_attended: bfloat16 [8, 64, 2, 128, 1024], P('dp', 'nbr', None, 'mp'), may hold values from -6 to 6
- query_w: bfloat16 [1024, 512], P(('nbr', 'mp')), may hold values from -0.1875 to 0.1875
- kv_w: bfloat16 [4096, 1024], P(('nbr', 'mp')), may hold values from -0.09375 to 0.09375
- out_w: bfloat16 [512, 1024], P(('nbr', 'mp')), may hold values from -0.25 to 0.25
- pos_bias: float32 [8, 128, 64], replicated, may hold values from -8 to 330
Outputs:
- attended: bfloat16 [8, 64, 2, 128, 1024], P('dp', 'nbr', None, 'mp')
- grad_rows: bfloat16 [8, 4096, 4096], P('dp', ('nbr', 'mp'))
- grad_neigh: bfloat16 [8, 128, 128, 1024], P('dp', 'nbr', 'mp')
- grad_query_w: float32 [1024, 512], P(('nbr', 'mp'))
- grad_out_w: float32 [512, 1024], P(('nbr', 'mp'))
Inputs may be any that keep to these rules, and one draw needn't show every extreme that they name: `owner_shift`: within one batch row the 8 shifts are all different.
All inputs are finite; a program needn't handle non-finite values.
Results may differ from a plain program's by a relative error of at most 0.013.
Values may be sent and summed in bfloat16 or wider, within the bound.
A program may use at most 128 MiB of HBM per device.

v0:
```python
import jax
import jax.numpy as jnp
from jax import lax
from jax.sharding import PartitionSpec as P


def attend(neighbours, kv_slots, cot_slots, score_bias, query_full, out_full, head_count):
    slot_count, span_rows, enc_width = neighbours.shape
    stretch_rows = kv_slots.shape[1]
    attn_width = query_full.shape[1]
    head_dim = attn_width // head_count
    flat_neigh = neighbours.reshape(slot_count * span_rows, enc_width)
    queries = jnp.dot(flat_neigh, query_full, preferred_element_type=jnp.float32).astype(
        jnp.bfloat16
    )
    query_heads = queries.reshape(slot_count, span_rows, head_count, head_dim)
    key_heads = kv_slots[:, :, :attn_width].reshape(slot_count, stretch_rows, head_count, head_dim)
    value_heads = kv_slots[:, :, attn_width:].reshape(
        slot_count, stretch_rows, head_count, head_dim
    )
    scores = jnp.einsum(
        "sihd,sjhd->shij", query_heads, key_heads, preferred_element_type=jnp.float32
    )
    scores = scores * 0.125 + score_bias[None]
    row_max = jnp.max(scores, axis=-1, keepdims=True)
    scaled = jnp.exp(scores - row_max)
    weights = scaled / jnp.sum(scaled, axis=-1, keepdims=True)
    probabilities = weights.astype(jnp.bfloat16)
    mixture = jnp.einsum(
        "shij,sjhd->sihd", probabilities, value_heads, preferred_element_type=jnp.float32
    )
    mixture = mixture.astype(jnp.bfloat16).reshape(slot_count * span_rows, attn_width)
    result = jnp.dot(mixture, out_full, preferred_element_type=jnp.float32).astype(jnp.bfloat16)
    result = result.reshape(slot_count, span_rows, enc_width)
    cot_flat = cot_slots.reshape(slot_count * span_rows, enc_width)
    grad_mixture = jnp.dot(cot_flat, out_full.T, preferred_element_type=jnp.float32).astype(
        jnp.bfloat16
    )
    grad_out = jnp.dot(mixture.T, cot_flat, preferred_element_type=jnp.float32)
    grad_heads = grad_mixture.reshape(slot_count, span_rows, head_count, head_dim)
    grad_probs = jnp.einsum(
        "sihd,sjhd->shij", grad_heads, value_heads, preferred_element_type=jnp.float32
    )
    grad_scores = weights * (grad_probs - jnp.sum(grad_probs * weights, axis=-1, keepdims=True))
    grad_scores = grad_scores.astype(jnp.bfloat16)
    grad_queries = jnp.einsum(
        "shij,sjhd->sihd", grad_scores, key_heads, preferred_element_type=jnp.float32
    )
    grad_queries = (
        (grad_queries * 0.125).astype(jnp.bfloat16).reshape(slot_count * span_rows, attn_width)
    )
    grad_neigh = jnp.dot(grad_queries, query_full.T, preferred_element_type=jnp.float32).astype(
        jnp.bfloat16
    )
    grad_neigh = grad_neigh.reshape(slot_count, span_rows, enc_width)
    grad_query = jnp.dot(flat_neigh.T, grad_queries, preferred_element_type=jnp.float32)
    grad_keys = (
        jnp.einsum("shij,sihd->sjhd", grad_scores, query_heads, preferred_element_type=jnp.float32)
        * 0.125
    )
    grad_values = jnp.einsum(
        "shij,sihd->sjhd", probabilities, grad_heads, preferred_element_type=jnp.float32
    )
    grad_kv = jnp.concatenate(
        [
            grad_keys.reshape(slot_count, stretch_rows, attn_width),
            grad_values.reshape(slot_count, stretch_rows, attn_width),
        ],
        axis=-1,
    )
    return (result, grad_kv.astype(jnp.bfloat16), grad_neigh, grad_query, grad_out)


def select(form, table, data):
    return jnp.einsum(form, table, data, preferred_element_type=jnp.float32).astype(jnp.bfloat16)


def project_sum(summed, kv_full):
    high = lax.optimization_barrier(summed.astype(jnp.bfloat16))
    low = (summed - high.astype(jnp.float32)).astype(jnp.bfloat16)
    first = jnp.einsum("rf,df->rd", high, kv_full, preferred_element_type=jnp.float32)
    return first + jnp.einsum("rf,df->rd", low, kv_full, preferred_element_type=jnp.float32)


def local(dec_rows, owner_shift, nbr_rows, cot_attended, query_w, kv_w, out_w, pos_bias):
    groups = lax.axis_size("nbr")
    mp_count = lax.axis_size("mp")
    my_index = lax.axis_index("nbr")
    my_part = lax.axis_index("mp")
    query_full, kv_full, out_full = (
        lax.all_gather(query_w, ("nbr", "mp"), axis=0, tiled=True),
        lax.all_gather(kv_w, ("nbr", "mp"), axis=0, tiled=True),
        lax.all_gather(out_w, ("nbr", "mp"), axis=0, tiled=True),
    )
    tokens = dec_rows[0]
    rows_count, row_width = tokens.shape
    head_count = pos_bias.shape[0]
    stretch_rows = pos_bias.shape[2]
    stretches = rows_count // stretch_rows
    neigh_count = cot_attended.shape[2]
    slot_count = stretches * neigh_count
    neighbours = nbr_rows[0]
    span_rows = neighbours.shape[1]
    score_bias = lax.dynamic_slice_in_dim(pos_bias, my_part * span_rows, span_rows, 1)
    keys_vals = jnp.dot(tokens, kv_full, preferred_element_type=jnp.float32).astype(jnp.bfloat16)
    kv_stretches = keys_vals.reshape(stretches, stretch_rows, keys_vals.shape[1])
    shifts = owner_shift[0].reshape(slot_count)
    peer_ids = jnp.arange(groups, dtype=jnp.int32)
    outward = (shifts[None, :] == (peer_ids[:, None] - my_index) % groups).astype(jnp.bfloat16)
    inward = (peer_ids[None, :] == (my_index - shifts[:, None]) % groups).astype(jnp.bfloat16)
    outward_three = outward.reshape(groups, stretches, neigh_count)
    cot_local = cot_attended[0]
    send_kv = select("pck,cjf->pjf", outward_three, kv_stretches)
    send_cot = select("pck,ckif->pif", outward_three, cot_local)
    got_kv, got_cot = (
        lax.all_to_all(send_kv, "nbr", split_axis=0, concat_axis=0, tiled=True),
        lax.all_to_all(send_cot, "nbr", split_axis=0, concat_axis=0, tiled=True),
    )
    kv_slots = select("sp,pjf->sjf", inward, got_kv)
    cot_slots = select("sp,pif->sif", inward, got_cot)
    result, grad_kv, grad_neigh, grad_query, grad_out = attend(
        neighbours, kv_slots, cot_slots, score_bias, query_full, out_full, head_count
    )
    back_out = select("sp,sif->pif", inward, result)
    back_kv = select("sp,sjf->pjf", inward, grad_kv)
    got_out, got_grad = (
        lax.all_to_all(back_out, "nbr", split_axis=0, concat_axis=0, tiled=True),
        lax.all_to_all(back_kv, "nbr", split_axis=0, concat_axis=0, tiled=True),
    )
    attended = select("pck,pif->ckif", outward_three, got_out)
    kv_row_grads = select("pck,pjf->cjkf", outward_three, got_grad)
    kv_row_grads = kv_row_grads.reshape(rows_count, neigh_count, kv_row_grads.shape[3])
    row_grad = lax.psum_scatter(
        project_sum(jnp.sum(kv_row_grads.astype(jnp.float32), axis=1), kv_full).astype(
            jnp.bfloat16
        ),
        "mp",
        scatter_dimension=0,
        tiled=True,
    )
    grad_rows = row_grad[None]
    summed_query, summed_out = lax.psum((grad_query, grad_out), ("dp", "nbr", "mp"))
    place_index = my_index * mp_count + my_part
    query_rows = summed_query.shape[0] // (groups * mp_count)
    out_rows = summed_out.shape[0] // (groups * mp_count)
    grad_query_w = lax.dynamic_slice_in_dim(summed_query, place_index * query_rows, query_rows, 0)
    grad_out_w = lax.dynamic_slice_in_dim(summed_out, place_index * out_rows, out_rows, 0)
    return (attended[None], grad_rows, grad_neigh[None], grad_query_w, grad_out_w)


def solution(mesh):
    placed = (
        P("dp", "nbr", None),
        P("dp", None, None),
        P("dp", "nbr", "mp", None),
        P("dp", "nbr", None, "mp", None),
        P(("nbr", "mp"), None),
        P(("nbr", "mp"), None),
        P(("nbr", "mp"), None),
        P(),
    )
    return jax.shard_map(
        local,
        mesh=mesh,
        in_specs=placed,
        out_specs=(
            P("dp", "nbr", None, "mp", None),
            P("dp", ("nbr", "mp"), None),
            P("dp", "nbr", "mp", None),
            P(("nbr", "mp"), None),
            P(("nbr", "mp"), None),
        ),
        check_vma=False,
    )
```

profile of v0, /device:TPU:2, one launch (start us, length us, event | category | flops | bytes accessed | tf_op | source)
XLA Modules:
  0.0 700.6 jit_solution(18438296595055865100)
XLA Ops:
  8.7 2.7 bitcast_convert_fusion
  11.4 2.5 copy.65
  13.9 6.3 all-to-all-start.2
  21.0 104.3 %all-gather.4.cloned.1.call-done = bf16[4096,1024]{1,0:T(8,128)(2,1)} async-done(((bf16[128,1024]{1,0:T(8,128)(2,1)}), bf16[4096,1024]{1,0:T(8,128)(2,1)}) %all-gather.4.cloned.1.call-update) | async-done | bytes 8388624 | tf_op jit(solution)/shard_map/all_gather | solution.py:92
  125.3 5.7 fusion.32
  131.8 2.5 copy.54
  134.3 8.2 %all-to-all-start = ((bf16[16,64,1024]{2,1,0:T(8,128)(2,1)}), bf16[16,64,1024]{2,1,0:T(8,128)(2,1)S(1)}, u32[]{:S(2)}, u32[]{:S(2)}) async-start(bf16[16,64,1024]{2,1,0:T(8,128)(2,1)} %copy.54), calls=%async_computation | async-start | bytes 4194304 | tf_op jit(solution)/shard_map/all_to_all | solution.py:116
  142.8 2.9 fusion.17
  146.2 83.0 %all-gather.6.cloned.1.call-done = bf16[1024,512]{1,0:T(8,128)(2,1)} async-done(((bf16[32,512]{1,0:T(8,128)(2,1)}), bf16[1024,512]{1,0:T(8,128)(2,1)}) %all-gather.6.cloned.1.call-update) | async-done | bytes 1048592 | tf_op jit(solution)/shard_map/all_gather | solution.py:91
  229.2 3.0 convolution_convert_fusion.8
  237.1 79.8 %all-gather.8.cloned.1.call-done = bf16[512,1024]{1,0:T(8,128)(2,1)} async-done(((bf16[16,1024]{1,0:T(8,128)(2,1)}), bf16[512,1024]{1,0:T(8,128)(2,1)}) %all-gather.8.cloned.1.call-update) | async-done | bytes 1048592 | tf_op jit(solution)/shard_map/all_gather | solution.py:93
  316.9 2.8 convolution_convert_fusion.7
  322.0 2.6 copy.74
  332.3 3.7 convolution_convert_fusion.3
  336.0 2.7 copy.77
  338.7 3.2 multiply_reduce_fusion
  345.5 2.6 reshape.141
  352.5 5.6 all-to-all-start.3
  358.2 3.7 fusion.26
  362.0 2.6 copy.60
  364.6 2.6 reshape.128
  369.2 3.5 convolution_bitcast_fusion
  374.8 13.4 %all-to-all-done.3 = bf16[16,64,1024]{2,1,0:T(8,128)(2,1)} async-done(((bf16[16,64,1024]{2,1,0:T(8,128)(2,1)}), bf16[16,64,1024]{2,1,0:T(8,128)(2,1)}, u32[]{:S(2)}, u32[]{:S(2)}) %all-to-all-start.3) | async-done | bytes 2097184 | tf_op jit(solution)/shard_map/all_to_all | solution.py:128
  388.2 3.4 convert_reduce_fusion
  392.5 6.0 fusion.71
  398.6 3.7 fusion.1
  405.2 2.5 copy.62
  407.6 6.0 all-to-all-start.1
  415.4 28.9 %all-to-all-done.1 = bf16[16,64,1024]{2,1,0:T(8,128)(2,1)} async-done(((bf16[16,64,1024]{2,1,0:T(8,128)(2,1)}), bf16[16,64,1024]{2,1,0:T(8,128)(2,1)}, u32[]{:S(2)}, u32[]{:S(2)}) %all-to-all-start.1) | async-done | bytes 2097184 | tf_op jit(solution)/shard_map/all_to_all | solution.py:127
  444.3 3.2 fusion.29
  448.8 207.5 %all-reduce.3.cloned.1.call-done = (f32[1024,512]{0,1:T(8,128)}, f32[512,1024]{1,0:T(8,128)}) async-done(((f32[1024,512]{0,1:T(8,128)}, f32[512,1024]{1,0:T(8,128)}), (f32[1024,512]{0,1:T(8,128)}, f32[512,1024]{1,0:T(8,128)})) %all-reduce.3.cloned.1.call-update) | async-done | bytes 4194320 | tf_op jit(solution)/shard_map/psum | solution.py:142
  659.6 34.2 %reduce-scatter.2.cloned.1.call-done = bf16[128,4096]{1,0:T(8,128)(2,1)} async-done(((bf16[256,4096]{1,0:T(8,128)(2,1)}), bf16[128,4096]{1,0:T(8,128)(2,1)}) %reduce-scatter.2.cloned.1.call-update) | async-done | bytes 1048592 | tf_op jit(solution)/shard_map/reduce_scatter | solution.py:133
  (79 shorter events, 41.0 us)
Async XLA Ops:
  7.2 118.2 %copy-start = (bf16[1,256,4096]{2,1,0:T(8,128)(2,1)S(1)}, bf16[1,256,4096]{2,1,0:T(8,128)(2,1)}, u32[]{:S(2)}) copy-start(bf16[1,256,4096]{2,1,0:T(8,128)(2,1)} %param.8) | copy-start | bytes 6291460
  7.2 118.1 %all-gather.4.cloned.1.call-start = ((), (), s32[]{:S(2)}) async-start(), calls=%async_computation.5 | async-start | bytes 8650752 | tf_op jit(solution)/shard_map/all_gather | solution.py:92
  7.9 221.3 %all-gather.6.cloned.1.call-start = ((), (), s32[]{:S(2)}) async-start(), calls=%async_computation.6 | async-start | bytes 1081344 | tf_op jit(solution)/shard_map/all_gather | solution.py:91
  13.9 7.1 %copy-start.10 = (s32[1,4,2]{1,2,0:T(2,128)S(1)}, s32[1,4,2]{1,2,0:T(2,128)}, u32[]{:S(2)}) copy-start(s32[1,4,2]{1,2,0:T(2,128)} %param.9) | copy-start | bytes 100
  13.9 120.4 %all-to-all-start.2 = ((bf16[16,64,1024]{2,1,0:T(8,128)(2,1)}), bf16[16,64,1024]{2,1,0:T(8,128)(2,1)}, u32[]{:S(2)}, u32[]{:S(2)}) async-start(bf16[16,64,1024]{2,1,0:T(8,128)(2,1)} %copy.65), calls=%async_computation.2 | async-start | bytes 4194304 | tf_op jit(solution)/shard_map/all_to_all | solution.py:117
  20.2 296.7 %all-gather.8.cloned.1.call-start = ((), (), s32[]{:S(2)}) async-start(), calls=%async_computation.7 | async-start | bytes 1081344 | tf_op jit(solution)/shard_map/all_gather | solution.py:93
  134.3 8.4 %copy-start.9 = (f32[8,128,64]{1,2,0:T(8,128)S(1)}, f32[8,128,64]{1,2,0:T(8,128)}, u32[]{:S(2)}) copy-start(f32[8,128,64]{1,2,0:T(8,128)} %param.15) | copy-start | bytes 786436
  134.3 190.3 %all-to-all-start = ((bf16[16,64,1024]{2,1,0:T(8,128)(2,1)}), bf16[16,64,1024]{2,1,0:T(8,128)(2,1)S(1)}, u32[]{:S(2)}, u32[]{:S(2)}) async-start(bf16[16,64,1024]{2,1,0:T(8,128)(2,1)} %copy.54), calls=%async_computation | async-start | bytes 4194304 | tf_op jit(solution)/shard_map/all_to_all | solution.py:116
  326.8 3.2 copy-start.2
  332.3 6.4 copy-start.8
  338.7 3.2 copy-start.7
  341.9 1.2 copy-start.3
  352.5 35.7 %all-to-all-start.3 = ((bf16[16,64,1024]{2,1,0:T(8,128)(2,1)}), bf16[16,64,1024]{2,1,0:T(8,128)(2,1)}, u32[]{:S(2)}, u32[]{:S(2)}) async-start(bf16[16,64,1024]{2,1,0:T(8,128)(2,1)} %copy.78), calls=%async_computation.3 | async-start | bytes 4194304 | tf_op jit(solution)/shard_map/all_to_all | solution.py:128
  358.2 298.1 %all-reduce.3.cloned.1.call-start = ((), (), s32[]{:S(2)}) async-start(), calls=%async_computation.9 | async-start | bytes 8388608 | tf_op jit(solution)/shard_map/psum | solution.py:142
  369.2 5.5 copy-start.4
  369.2 3.5 copy-start.6
  374.7 319.1 %reduce-scatter.2.cloned.1.call-start = ((), (), s32[]{:S(2)}) async-start(), calls=%async_computation.8 | async-start | bytes 3145728 | tf_op jit(solution)/shard_map/reduce_scatter | solution.py:133
  392.3 6.2 slice-start
  392.5 6.0 slice-start.1
  402.3 1.2 copy-start.12
  407.6 6.0 copy-start.5
  407.6 6.0 copy-start.11
  407.6 36.7 %all-to-all-start.1 = ((bf16[16,64,1024]{2,1,0:T(8,128)(2,1)}), bf16[16,64,1024]{2,1,0:T(8,128)(2,1)}, u32[]{:S(2)}, u32[]{:S(2)}) async-start(bf16[16,64,1024]{2,1,0:T(8,128)(2,1)} %copy.62), calls=%async_computation.1 | async-start | bytes 4194304 | tf_op jit(solution)/shard_map/all_to_all | solution.py:127
  444.3 249.5 %copy-start.1 = (bf16[1,256,4096]{2,1,0:T(8,128)(2,1)S(1)}, bf16[1,256,4096]{2,1,0:T(8,128)(2,1)}, u32[]{:S(2)}) copy-start(bf16[1,256,4096]{2,1,0:T(8,128)(2,1)} %param.8) | copy-start | bytes 6291460
Sparse Core Ops, SparseCore 0:
  9.8 115.4 all-gather.3
  127.1 102.0 all-gather.5
  231.1 85.7 all-gather.7
  374.8 281.3 all-reduce.2
  659.4 34.4 reduce-scatter.1
where the time goes:
time: 709 us; the launch traced here: 701 us
  waiting for transfers between devices  553 us (78%)
  matrix products  60.7 us (9%)
  local copies, waits for them, and re-layouts  45 us (6%)
  starting transfers between devices  26.3 us (4%)
  between operations  14.4 us (2%)
    psum x1, waiting for transfers between devices, local(): lax.psum((grad_query, grad_out), ('dp', 'nbr', 'mp'))  207 us
    all_gather x1, waiting for transfers between devices, local(): lax.all_gather(kv_w, ('nbr', 'mp'), axis=0, tiled=True)  104 us
    all_gather x1, waiting for transfers between devices, local(): lax.all_gather(query_w, ('nbr', 'mp'), axis=0, tiled=True)  83 us
    all_gather x1, waiting for transfers between devices, local(): lax.all_gather(out_w, ('nbr', 'mp'), axis=0, tiled=True)  79.8 us
    reduce_scatter x1, waiting for transfers between devices, local(): lax.psum_scatter(project_sum(jnp.sum(kv_row_grads.astype(jnp.float32), ax...  34.2 us
    all_to_all x1, waiting for transfers between devices, local(): lax.all_to_all(back_out, 'nbr', split_axis=0, concat_axis=0, tiled=True)  28.9 us
    dot_general x8, matrix products, select(): jnp.einsum(form, table, data, preferred_element_type=jnp.float32)  17.1 us
  transfers between devices with their start and end apart: 9, of which 7 were waited for; matrix products, arithmetic and copies ran while one was open for 11% of the time, Pallas kernels for 0%

commit v1 on v0

v1 whole, which is shorter than its diff:
```python
import jax
import jax.numpy as jnp
from jax import lax
from jax.experimental import pallas as pl
from jax.experimental.pallas import tpu as pltpu
from jax.sharding import PartitionSpec as P

BF = jnp.bfloat16
F32 = jnp.float32
MESH = pl.DeviceIdType.MESH


def dot_nn(a, b):
    return lax.dot_general(a, b, (((1,), (0,)), ((), ())), preferred_element_type=F32)


def dot_nt(a, b):
    return lax.dot_general(a, b, (((1,), (1,)), ((), ())), preferred_element_type=F32)


def dot_tn(a, b):
    return lax.dot_general(a, b, (((0,), (0,)), ((), ())), preferred_element_type=F32)


def kernel(
    shift, dec_h, nbr_h, cot_h, wq_h, wkv_h, wo_h, bias_h,
    att_o, rows_o, neigh_o, gqw_o, gow_o,
    qw, kvw, ow, dec, nbr, nbr_t, cot, bias_raw, bias_t,
    queries, qs, qr, kv, gmix, mix, gq_loc, gs, gr, gq_all,
    gkv, gkv_s, gkv_r, att, rows, neigh,
    wred, ored, wr1, or1, wa1, oa1, wr2, or2, wa2, oa2, wr3, or3, zs, zr, za, zg, gqw_v, gow_v,
    lsem, ag_s, ag_r, qx_s, qx_r, gx_s, gx_r, mp_s, mp_r,
    r1_s, r1_r, r2_s, r2_r, r3_s, r3_r, r4_s, r4_r, r5_s, r5_r, osem,
):
    z = lax.axis_index("dp")
    n = lax.axis_index("nbr")
    m = lax.axis_index("mp")
    xh = n // 8
    y = (n // 2) % 4
    c = n % 2
    x = xh * 2 + m

    def at_y(j):
        return {"nbr": xh * 8 + ((y + j) % 4) * 2 + c}

    def at_x(j):
        far = (x + j) % 4
        return {"nbr": (far // 2) * 8 + y * 2 + c, "mp": far % 2}

    def at_z(j):
        return {"dp": (z + j) % 8}

    def at_n(j):
        return {"nbr": (n + j) % 16}

    at_core = {"nbr": xh * 8 + y * 2 + (1 - c)}
    at_mp = {"mp": 1 - m}

    def remote(src, dst, ssem, rsem, device):
        return pltpu.make_async_remote_copy(
            src_ref=src, dst_ref=dst, send_sem=ssem, recv_sem=rsem, device_id=device, device_id_type=MESH
        )

    def each(lo, hi, body):
        lax.fori_loop(lo, hi, lambda j, carry: (body(j), carry)[1], 0)

    local_in = [
        pltpu.make_async_copy(wq_h, qw.at[xh, y, c, m], lsem.at[0]),
        pltpu.make_async_copy(wo_h, ow.at[xh, y, c, m], lsem.at[1]),
        pltpu.make_async_copy(wkv_h, kvw.at[xh, y, c, m], lsem.at[2]),
        pltpu.make_async_copy(nbr_h, nbr, lsem.at[3]),
        pltpu.make_async_copy(cot_h, cot, lsem.at[4]),
        pltpu.make_async_copy(dec_h, dec, lsem.at[5]),
        pltpu.make_async_copy(bias_h, bias_raw, lsem.at[6]),
    ]
    for one in local_in:
        one.start()

    barrier = pltpu.get_barrier_semaphore()
    each(1, 16, lambda j: pl.semaphore_signal(barrier, inc=1, device_id=at_n(j), device_id_type=MESH))
    each(1, 8, lambda j: pl.semaphore_signal(barrier, inc=1, device_id=at_z(j), device_id_type=MESH))
    pl.semaphore_signal(barrier, inc=1, device_id=at_x(1), device_id_type=MESH)
    pl.semaphore_signal(barrier, inc=1, device_id=at_x(3), device_id_type=MESH)
    pl.semaphore_wait(barrier, 24)

    every = slice(None)
    halves = [
        (qw, [(pl.ds(0, 16), every), (pl.ds(16, 16), every)]),
        (ow, [(every, pl.ds(0, 512)), (every, pl.ds(512, 512))]),
        (kvw, [(pl.ds(0, 64), every), (pl.ds(64, 64), every)]),
    ]

    def first(t, h, j, arriving):
        buf, parts = halves[t]
        sy, sx, sm = y, xh, m
        if arriving:
            if h == 0:
                sy = (y + 4 - j) % 4
            else:
                far = (x + 4 - j) % 4
                sx, sm = far // 2, far % 2
        ref = buf.at[(sx, sy, c, sm) + parts[h]]
        return remote(ref, ref, ag_s.at[t, 0, h, j], ag_r.at[t, 0, h, j], at_y(j) if h == 0 else at_x(j))

    def second(t, h, j, arriving):
        buf, parts = halves[t]
        if h == 0:
            far = (x + 4 - j) % 4 if arriving else x
            ref = buf.at[(far // 2, every, c, far % 2) + parts[h]]
        else:
            sy = (y + 4 - j) % 4 if arriving else y
            ref = buf.at[(every, sy, c, every) + parts[h]]
        return remote(ref, ref, ag_s.at[t, 1, h, j], ag_r.at[t, 1, h, j], at_x(j) if h == 0 else at_y(j))

    def third(t, arriving):
        buf = halves[t][0]
        ref = buf.at[:, :, (1 - c) if arriving else c]
        return remote(ref, ref, ag_s.at[t, 2, 0, 0], ag_r.at[t, 2, 0, 0], at_core)

    for t in range(3):
        local_in[t].wait()
        for h in range(2):
            each(1, 4, lambda j, t=t, h=h: first(t, h, j, False).start())

    local_in[3].wait()
    nbr_t[...] = nbr[...].T
    for t in range(3):
        for h in range(2):
            each(1, 4, lambda j, t=t, h=h: first(t, h, j, True).wait_recv())
            each(1, 4, lambda j, t=t, h=h: second(t, h, j, False).start())
    for h in range(2):
        each(1, 4, lambda j, h=h: second(0, h, j, True).wait_recv())
    third(0, False).start()
    third(0, True).wait_recv()

    def query_block(i):
        r = pl.ds(pl.multiple_of(i * 128, 128), 128)
        found = dot_nn(nbr[r, :], qw[...].reshape(1024, 512)).astype(BF)
        queries[pl.ds(2 * i, 2)] = found.reshape(2, 64, 512)

    each(0, 4, query_block)

    def slot_of(t):
        found = 0
        for s in range(8):
            found = found + jnp.where(shift[s % 2, s // 2] == t, s, 0)
        return jnp.minimum(found, 7)

    def query_send(t):
        qs[t] = queries[slot_of(t)]
        remote(qs.at[t], qr.at[t], qx_s.at[t], qx_r.at[t], at_n(16 - t)).start()

    each(1, 16, query_send)
    qr[0] = queries[slot_of(0)]

    local_in[6].wait()
    for h in range(8):
        turned = bias_raw[h]
        rolled = pltpu.roll(turned, 64, 1)
        lane = lax.broadcasted_iota(jnp.int32, (64, 128), 1)
        keep = (lane < 64) == (m == 0)
        bias_t[h * 64 : (h + 1) * 64, :] = jnp.where(keep, turned, rolled)

    for h in range(2):
        each(1, 4, lambda j, h=h: second(1, h, j, True).wait_recv())
    third(1, False).start()
    third(1, True).wait_recv()
    local_in[4].wait()

    def gmix_block(i):
        r = pl.ds(pl.multiple_of(i * 128, 128), 128)
        gmix[r, :] = dot_nt(cot[r, :], ow[...].reshape(512, 1024)).astype(BF)

    each(0, 4, gmix_block)

    for h in range(2):
        each(1, 4, lambda j, h=h: second(2, h, j, True).wait_recv())
    third(2, False).start()
    local_in[5].wait()
    third(2, True).wait_recv()

    gkv[...] = jnp.zeros_like(gkv)

    def kv_block(i):
        cols = pl.ds(pl.multiple_of(i * 512, 512), 512)
        gkv[...] += dot_nn(dec[:, cols], kvw[i // 4, i % 4].reshape(512, 1024))

    each(0, 8, kv_block)
    kv[...] = gkv[...].astype(BF)

    each(1, 16, lambda t: remote(qr.at[t], qr.at[t], qx_s.at[t], qx_r.at[t], at_n(t)).wait_recv())

    row_head = lax.broadcasted_iota(jnp.int32, (256, 256), 0) // 64
    col_head = lax.broadcasted_iota(jnp.int32, (256, 256), 1) // 64
    same = row_head == col_head

    def spread(block):
        return jnp.where(same, jnp.concatenate([block] * 4, axis=0), jnp.zeros((), BF))

    def gather_diag(full):
        kept = jnp.where(same, full, 0.0)
        return kept[0:64] + kept[64:128] + kept[128:192] + kept[192:256]

    def stretch(i):
        s = (i + 2 * (1 - m)) % 4
        q_both = jnp.concatenate([qr[shift[0, s]], qr[shift[1, s]]], axis=0)
        rows_kv = pl.ds(pl.multiple_of(s * 64, 64), 64)
        rows_tok = pl.ds(pl.multiple_of(s * 128, 128), 128)
        for g in range(2):
            lo, hi = g * 256, (g + 1) * 256
            keys = spread(kv[rows_kv, lo:hi])
            vals = spread(kv[rows_kv, 512 + lo : 512 + hi])
            q = q_both[:, lo:hi]
            gm = gmix[rows_tok, lo:hi]
            score = dot_nt(keys, q) * 0.125 + bias_t[lo:hi, :]
            grad_p = dot_nt(vals, gm)
            score = score.reshape(4, 64, 128)
            grad_p = grad_p.reshape(4, 64, 128)
            top = jnp.max(score, axis=1, keepdims=True)
            e = jnp.exp(score - top)
            w = e * (1.0 / jnp.sum(e, axis=1, keepdims=True))
            probs = w.astype(BF).reshape(256, 128)
            inner = jnp.sum(w * grad_p, axis=1, keepdims=True)
            gscore = (w * (grad_p - inner)).astype(BF).reshape(256, 128)
            mix[rows_tok, lo:hi] = dot_tn(probs, vals).astype(BF)
            gq = (dot_tn(gscore, keys) * 0.125).astype(BF)
            gq_loc[pl.ds(2 * s, 2), :, lo:hi] = gq.reshape(2, 64, 256)
            gkv[rows_kv, lo:hi] = gather_diag(dot_nn(gscore, q)) * 0.125
            gkv[rows_kv, 512 + lo : 512 + hi] = gather_diag(dot_nn(probs, gm))

    each(0, 2, stretch)
    gkv_s[...] = gkv[pl.ds(pl.multiple_of((1 - m) * 128, 128), 128), :].astype(BF)
    mp_copy = remote(gkv_s, gkv_r, mp_s.at[0], mp_r.at[0], at_mp)
    mp_copy.start()
    each(2, 4, stretch)

    def grad_send(t):
        gs[t] = gq_loc[slot_of(t)]
        remote(gs.at[t], gr.at[t], gx_s.at[t], gx_r.at[t], at_n(t)).start()

    each(1, 16, grad_send)
    gr[0] = gq_loc[slot_of(0)]

    mix_t = mix[...].T
    for p in range(2):
        block = dot_nn(mix_t[p * 256 : (p + 1) * 256], cot[...])
        ored[p] = block.astype(BF).reshape(4, 2, 2, 16, 1024)
    o1 = remote(ored.at[:, :, 1 - c], or1, r1_s.at[0], r1_r.at[0], at_core)
    o1.start()

    def att_block(i):
        r = pl.ds(pl.multiple_of(i * 128, 128), 128)
        att[r, :] = dot_nn(mix[r, :], ow[...].reshape(512, 1024)).astype(BF)

    each(0, 4, att_block)
    out_att = pltpu.make_async_copy(att, att_o, osem.at[0])
    out_att.start()

    o1.wait_recv()
    oa1[...] = (ored[:, :, c].astype(F32) + or1[...].astype(F32)).astype(BF)

    def o2(j):
        return remote(
            oa1.at[:, (y + j) % 4], or2.at[j], r2_s.at[0, j], r2_r.at[0, j], at_y(j)
        )

    each(1, 4, lambda j: o2(j).start())

    mp_copy.wait_recv()
    mine = pl.ds(pl.multiple_of(m * 128, 128), 128)
    kv_sum = (gkv[mine, :] + gkv_r[...].astype(F32)).astype(BF)
    gkv_s2 = kv_sum

    def rows_block(i):
        cols = pl.ds(pl.multiple_of(i * 512, 512), 512)
        rows[:, cols] = dot_nt(gkv_s2, kvw[i // 4, i % 4].reshape(512, 1024)).astype(BF)

    each(0, 8, rows_block)
    out_rows = pltpu.make_async_copy(rows, rows_o, osem.at[1])
    out_rows.start()

    each(1, 4, lambda j: o2(j).wait_recv())
    oa2[...] = (
        oa1[:, y].astype(F32) + or2[1].astype(F32) + or2[2].astype(F32) + or2[3].astype(F32)
    ).astype(BF)

    def o3(j):
        far = (x + j) % 4
        return remote(oa2.at[far // 2, far % 2], or3.at[j], r3_s.at[0, j], r3_r.at[0, j], at_x(j))

    each(1, 4, lambda j: o3(j).start())

    each(1, 16, lambda t: remote(gr.at[t], gr.at[t], gx_s.at[t], gx_r.at[t], at_n(t)).wait_recv())
    for s in range(8):
        gq_all[s * 64 : (s + 1) * 64, :] = gr[shift[s % 2, s // 2]]

    for p in range(2):
        block = dot_nn(nbr_t[p * 512 : (p + 1) * 512, :], gq_all[...])
        wred[p] = block.astype(BF).reshape(4, 2, 2, 32, 512)
    w1 = remote(wred.at[:, :, 1 - c], wr1, r1_s.at[1], r1_r.at[1], at_core)
    w1.start()

    def neigh_block(i):
        r = pl.ds(pl.multiple_of(i * 128, 128), 128)
        neigh[r, :] = dot_nt(gq_all[r, :], qw[...].reshape(1024, 512)).astype(BF)

    w1.wait_recv()
    wa1[...] = (wred[:, :, c].astype(F32) + wr1[...].astype(F32)).astype(BF)

    def w2(j):
        return remote(
            wa1.at[:, (y + j) % 4], wr2.at[j], r2_s.at[1, j], r2_r.at[1, j], at_y(j)
        )

    each(1, 4, lambda j: w2(j).start())
    each(0, 4, neigh_block)
    out_neigh = pltpu.make_async_copy(neigh, neigh_o, osem.at[2])
    out_neigh.start()
    each(1, 4, lambda j: w2(j).wait_recv())
    wa2[...] = (
        wa1[:, y].astype(F32) + wr2[1].astype(F32) + wr2[2].astype(F32) + wr2[3].astype(F32)
    ).astype(BF)

    def w3(j):
        far = (x + j) % 4
        return remote(wa2.at[far // 2, far % 2], wr3.at[j], r3_s.at[1, j], r3_r.at[1, j], at_x(j))

    each(1, 4, lambda j: w3(j).start())
    each(1, 4, lambda j: o3(j).wait_recv())
    o_sum = (
        oa2[xh, m].astype(F32) + or3[1].astype(F32) + or3[2].astype(F32) + or3[3].astype(F32)
    )
    each(1, 4, lambda j: w3(j).wait_recv())
    w_sum = (
        wa2[xh, m].astype(F32) + wr3[1].astype(F32) + wr3[2].astype(F32) + wr3[3].astype(F32)
    )
    for p in range(8):
        zs[p, 0:16] = w_sum[(p // 4) * 16 : (p // 4) * 16 + 16, (p % 4) * 128 : (p % 4) * 128 + 128].astype(BF)
        zs[p, 16:32] = o_sum[:, p * 128 : (p + 1) * 128].astype(BF)

    def z1(j):
        return remote(zs.at[(z + j) % 8], zr.at[j], r4_s.at[j], r4_r.at[j], at_z(j))

    each(1, 8, lambda j: z1(j).start())
    total = zs[z].astype(F32)
    each(1, 8, lambda j: z1(j).wait_recv())
    for j in range(1, 8):
        total = total + zr[j].astype(F32)
    za[...] = total.astype(BF)

    def z2(j, arriving):
        place = (z + 8 - j) % 8 if arriving else z
        return remote(za, zg.at[place], r5_s.at[j], r5_r.at[j], at_z(j))

    each(1, 8, lambda j: z2(j, False).start())
    zg[z] = za[...]
    each(1, 8, lambda j: z2(j, True).wait_recv())
    for p in range(8):
        gqw_v[(p // 4) * 16 : (p // 4) * 16 + 16, (p % 4) * 128 : (p % 4) * 128 + 128] = zg[p, 0:16].astype(F32)
        gow_v[:, p * 128 : (p + 1) * 128] = zg[p, 16:32].astype(F32)
    out_q = pltpu.make_async_copy(gqw_v, gqw_o, osem.at[3])
    out_o = pltpu.make_async_copy(gow_v, gow_o, osem.at[4])
    out_q.start()
    out_o.start()

    for t in range(3):
        for h in range(2):
            each(1, 4, lambda j, t=t, h=h: first(t, h, j, False).wait_send())
            each(1, 4, lambda j, t=t, h=h: second(t, h, j, False).wait_send())
        third(t, False).wait_send()
    each(1, 16, lambda t: remote(qs.at[t], qr.at[t], qx_s.at[t], qx_r.at[t], at_n(t)).wait_send())
    each(1, 16, lambda t: remote(gs.at[t], gr.at[t], gx_s.at[t], gx_r.at[t], at_n(t)).wait_send())
    mp_copy.wait_send()
    o1.wait_send()
    w1.wait_send()
    each(1, 4, lambda j: o2(j).wait_send())
    each(1, 4, lambda j: w2(j).wait_send())
    each(1, 4, lambda j: o3(j).wait_send())
    each(1, 4, lambda j: w3(j).wait_send())
    each(1, 8, lambda j: z1(j).wait_send())
    each(1, 8, lambda j: z2(j, False).wait_send())
    out_att.wait()
    out_rows.wait()
    out_neigh.wait()
    out_q.wait()
    out_o.wait()


def local(dec_rows, owner_shift, nbr_rows, cot_attended, query_w, kv_w, out_w, pos_bias):
    vmem = pltpu.VMEM
    dma = pltpu.SemaphoreType.DMA
    anywhere = pl.BlockSpec(memory_space=pl.ANY)
    scratch = [
        vmem((2, 4, 2, 2, 32, 512), BF), vmem((2, 4, 2, 2, 128, 1024), BF), vmem((2, 4, 2, 2, 16, 1024), BF),
        vmem((256, 4096), BF), vmem((512, 1024), BF), vmem((1024, 512), BF), vmem((512, 1024), BF),
        vmem((8, 64, 128), F32), vmem((512, 128), F32),
        vmem((8, 64, 512), BF), vmem((16, 64, 512), BF), vmem((16, 64, 512), BF), vmem((256, 1024), BF),
        vmem((512, 512), BF), vmem((512, 512), BF), vmem((8, 64, 512), BF),
        vmem((16, 64, 512), BF), vmem((16, 64, 512), BF), vmem((512, 512), BF),
        vmem((256, 1024), F32), vmem((128, 1024), BF), vmem((128, 1024), BF),
        vmem((512, 1024), BF), vmem((128, 4096), BF), vmem((512, 1024), BF),
        vmem((2, 4, 2, 2, 32, 512), BF), vmem((2, 4, 2, 2, 16, 1024), BF),
        vmem((2, 4, 2, 32, 512), BF), vmem((2, 4, 2, 16, 1024), BF),
        vmem((2, 4, 2, 32, 512), BF), vmem((2, 4, 2, 16, 1024), BF),
        vmem((4, 2, 2, 32, 512), BF), vmem((4, 2, 2, 16, 1024), BF),
        vmem((2, 2, 32, 512), BF), vmem((2, 2, 16, 1024), BF),
        vmem((4, 32, 512), BF), vmem((4, 16, 1024), BF),
        vmem((8, 32, 128), BF), vmem((8, 32, 128), BF), vmem((32, 128), BF), vmem((8, 32, 128), BF),
        vmem((32, 512), F32), vmem((16, 1024), F32),
        dma((7,)), dma((3, 3, 2, 4)), dma((3, 3, 2, 4)), dma((16,)), dma((16,)), dma((16,)), dma((16,)),
        dma((1,)), dma((1,)), dma((2,)), dma((2,)), dma((2, 4)), dma((2, 4)), dma((2, 4)), dma((2, 4)),
        dma((8,)), dma((8,)), dma((8,)), dma((8,)), dma((5,)),
    ]
    attended, grad_rows, grad_neigh, grad_query_w, grad_out_w = pl.pallas_call(
        kernel,
        out_shape=(
            jax.ShapeDtypeStruct((512, 1024), BF),
            jax.ShapeDtypeStruct((128, 4096), BF),
            jax.ShapeDtypeStruct((512, 1024), BF),
            jax.ShapeDtypeStruct((32, 512), F32),
            jax.ShapeDtypeStruct((16, 1024), F32),
        ),
        in_specs=[pl.BlockSpec(memory_space=pltpu.SMEM)] + [anywhere] * 7,
        out_specs=[anywhere] * 5,
        scratch_shapes=scratch,
        compiler_params=pltpu.CompilerParams(
            collective_id=0, has_side_effects=True, vmem_limit_bytes=60 * 2**20
        ),
        cost_estimate=pl.CostEstimate(flops=7 * 10**9, bytes_accessed=12 * 2**20, transcendentals=2 * 10**6),
        name="retrieval",
    )(
        owner_shift[0].T,
        dec_rows[0],
        nbr_rows.reshape(512, 1024),
        cot_attended.reshape(512, 1024),
        query_w,
        kv_w,
        out_w,
        jnp.swapaxes(pos_bias, 1, 2),
    )
    return (
        attended.reshape(1, 4, 2, 64, 1024),
        grad_rows[None],
        grad_neigh.reshape(1, 8, 64, 1024),
        grad_query_w,
        grad_out_w,
    )


def solution(mesh):
    placed = (
        P("dp", "nbr", None),
        P("dp", None, None),
        P("dp", "nbr", "mp", None),
        P("dp", "nbr", None, "mp", None),
        P(("nbr", "mp"), None),
        P(("nbr", "mp"), None),
        P(("nbr", "mp"), None),
        P(),
    )
    return jax.shard_map(
        local,
        mesh=mesh,
        in_specs=placed,
        out_specs=(
            P("dp", "nbr", None, "mp", None),
            P("dp", ("nbr", "mp"), None),
            P("dp", "nbr", "mp", None),
            P(("nbr", "mp"), None),
            P(("nbr", "mp"), None),
        ),
        check_vma=False,
    )
```

time: 709 us -> 120 us (0.17); the launches traced: 701 us -> 120 us
  waiting for transfers between devices: 553 us -> 0 us
  Pallas kernels: 0 us -> 113 us
  matrix products: 60.7 us -> 0 us
  local copies, waits for them, and re-layouts: 45 us -> 5.62 us
  starting transfers between devices: 26.3 us -> 0 us
  between operations: 14.4 us -> 0.66 us
    all_gather x3 -> x0, waiting for transfers between devices: 267 us -> none  [the longest x1 104 us: local(): lax.all_gather(kv_w, ('nbr', 'mp'), axis=0, tiled=True)]
    psum x1 -> x0, waiting for transfers between devices: 207 us -> none  [local(): lax.psum((grad_query, grad_out), ('dp', 'nbr', 'mp'))]
    pallas_call x0 -> x1, Pallas kernels: none -> 113 us  [local(): pl.pallas_call(kernel, out_shape=(jax.ShapeDtypeStruct((512, 1024), BF),...]
    dot_general x22 -> x0, matrix products: 58.3 us -> none  [the longest x8 17.1 us: select(): jnp.einsum(form, table, data, preferred_element_type=jnp.float32)]
    all_to_all x4 -> x0, waiting for transfers between devices: 42.4 us -> none  [the longest x1 28.9 us: local(): lax.all_to_all(back_out, 'nbr', split_axis=0, concat_axis=0, tiled=True)]
    reduce_scatter x1 -> x0, waiting for transfers between devices: 34.2 us -> none  [local(): lax.psum_scatter(project_sum(jnp.sum(kv_row_grads.astype(jnp.float32), ax...]
    all_to_all x4 -> x0, starting transfers between devices: 26.1 us -> none  [the longest x1 8.16 us: local(): lax.all_to_all(send_kv, 'nbr', split_axis=0, concat_axis=0, tiled=True)]
    reshape x11 -> x0, local copies, waits for them, and re-layouts: 23 us -> none  [the longest x2 4.92 us: attend(): grad_mixture.reshape(slot_count, span_rows, head_count, head_dim)]
  transfers between devices with their start and end apart: 9 -> 0, of which waited for: 7 -> 0; matrix products, arithmetic and copies ran while one was open for 11% -> 0% of each run, Pallas kernels for 0% -> 0%
where the time goes in v1:
time: 120 us
  Pallas kernels  113 us (94%)
  local copies, waits for them, and re-layouts  5.62 us (5%)
    pallas_call x1, Pallas kernels, local(): pl.pallas_call(kernel, out_shape=(jax.ShapeDtypeStruct((512, 1024), BF),...  113 us
    unnamed x13, local copies, waits for them, and re-layouts  5.62 us

profile of v1, /device:TPU:2, one launch (start us, length us, event | category | flops | bytes accessed | tf_op | source)
XLA Modules:
  0.0 119.6 jit_solution(4382918193630987727)
XLA Ops:
  0.6 113.3 %retrieval.1 = (bf16[512,1024]{1,0:T(8,128)(2,1)}, bf16[128,4096]{1,0:T(8,128)(2,1)}, bf16[512,1024]{1,0:T(8,128)(2,1)}, f32[32,512]{1,0:T(8,128)}, f32[16,1024]{1,0:T(8,128)}) custom-call(s32[2,4]{1,0:T(2,128)} %bitcast.17, bf16[256,4096]{1,0:T(8,128)(2,1)} %bitcast.13, bf16[512,1024]{1,0:T(8,128)(2,1)} %bitcast.14, bf16[512,1024]{1,0:T(8,128)(2,1)} %bitcast.15, ...), custom_call_target="tpu_custom_call" | custom-call | flops 7000000000 | bytes 12582912 | tf_op jit(solution)/shard_map/retrieval/pallas_call | solution.py:414
  114.0 0.0 copy-start.1
  114.0 0.0 copy-start
  114.0 2.4 %copy.18 = bf16[1,4,2,64,1024]{4,3,2,1,0:T(8,128)(2,1)} copy(bf16[1,4,2,64,1024]{4,3,2,1,0:T(8,128)(2,1)} %bitcast.12) | data formatting | bytes 2097152
  116.4 0.0 copy-done.1
  116.4 0.0 copy-start.3
  116.4 0.0 copy-start.2
  116.4 1.0 copy.19
  117.4 0.0 copy-done
  117.4 1.0 copy.20
  118.4 0.0 copy-done.3
  118.4 0.6 copy.21
  119.0 0.0 copy-done.2
  119.0 0.6 copy.22
Async XLA Ops:
  114.0 2.4 %copy-start.1 = (bf16[128,4096]{1,0:T(8,128)(2,1)S(1)}, bf16[128,4096]{1,0:T(8,128)(2,1)}, u32[]{:S(2)}) copy-start(bf16[128,4096]{1,0:T(8,128)(2,1)} %get-tuple-element.11) | copy-start | bytes 3145732
  114.0 3.4 %copy-start = (bf16[512,1024]{1,0:T(8,128)(2,1)S(1)}, bf16[512,1024]{1,0:T(8,128)(2,1)}, u32[]{:S(2)}) copy-start(bf16[512,1024]{1,0:T(8,128)(2,1)} %get-tuple-element.12) | copy-start | bytes 3145732
  116.4 1.9 %copy-start.3 = (f32[32,512]{1,0:T(8,128)S(1)}, f32[32,512]{1,0:T(8,128)}, u32[]{:S(2)}) copy-start(f32[32,512]{1,0:T(8,128)} %get-tuple-element.23) | copy-start | bytes 196612
  116.4 2.6 %copy-start.2 = (f32[16,1024]{1,0:T(8,128)S(1)}, f32[16,1024]{1,0:T(8,128)}, u32[]{:S(2)}) copy-start(f32[16,1024]{1,0:T(8,128)} %get-tuple-element.24) | copy-start | bytes 196612

commit v2 on v1

v2 whole, which is shorter than its diff:
```python
import jax
import jax.numpy as jnp
from jax import lax
from jax.experimental import pallas as pl
from jax.experimental.pallas import tpu as pltpu
from jax.sharding import PartitionSpec as P

BF = jnp.bfloat16
F32 = jnp.float32
MESH = pl.DeviceIdType.MESH


def dot_nn(a, b):
    return lax.dot_general(a, b, (((1,), (0,)), ((), ())), preferred_element_type=F32)


def dot_nt(a, b):
    return lax.dot_general(a, b, (((1,), (1,)), ((), ())), preferred_element_type=F32)


def dot_tn(a, b):
    return lax.dot_general(a, b, (((0,), (0,)), ((), ())), preferred_element_type=F32)


def kernel(
    shift, dec_h, nbr_h, cot_h, wq_h, wkv_h, wo_h, bias_h,
    att_o, rows_o, neigh_o, gqw_o, gow_o,
    qw, kvw, ow, dec, nbr, nbr_t, cot, bias_raw, bias_t,
    queries, qs, qr, kv, gmix, mix, gq_loc, gs, gr_a, gr_b, gq_all,
    gkv, gkv_s, gkv_r, kv_sum, att, rows, neigh,
    wred, ored, wr1, or1, wa1, oa1, wr2y, wr2x, or2, wa2y, wa2x, oa2, wr3, or3, zs, zr, za, zg, gqw_v, gow_v,
    lsem, ag_s, ag_r, kv_ss, kv_rs, kc_s, kc_r, c_ss, c_rs, z_ss, z_rs, kz_s, kz_r, qx_s, qx_r, gx_s, gx_r, mp_s, mp_r,
    r1_s, r1_r, r2_s, r2_r, r3_s, r3_r, r4_s, r4_r, r5_s, r5_r, osem,
):
    z = lax.axis_index("dp")
    n = lax.axis_index("nbr")
    m = lax.axis_index("mp")
    xh = n // 8
    y = (n // 2) % 4
    c = n % 2
    x = xh * 2 + m

    def at_y(j):
        return {"nbr": xh * 8 + ((y + j) % 4) * 2 + c}

    def at_x(j):
        far = (x + j) % 4
        return {"nbr": (far // 2) * 8 + y * 2 + c, "mp": far % 2}

    def at_z(j):
        return {"dp": (z + j) % 8}

    def at_n(j):
        return {"nbr": (n + j) % 16}

    at_core = {"nbr": xh * 8 + y * 2 + (1 - c)}
    at_mp = {"mp": 1 - m}

    def remote(src, dst, ssem, rsem, device):
        return pltpu.make_async_remote_copy(
            src_ref=src, dst_ref=dst, send_sem=ssem, recv_sem=rsem, device_id=device, device_id_type=MESH
        )

    def each(lo, hi, body):
        lax.fori_loop(lo, hi, lambda j, carry: (body(j), carry)[1], 0)

    every = slice(None)

    def piece(place):
        return pl.ds(pl.multiple_of((place // 2) * 16, 16), 16), pl.ds(pl.multiple_of((place % 2) * 512, 512), 512)

    mine_z = piece(z)
    lower = pl.ds(64, 64)

    local_in = [
        pltpu.make_async_copy(wq_h, qw.at[xh, y, c, m], lsem.at[0]),
        pltpu.make_async_copy(wo_h, ow.at[xh, y, c, m], lsem.at[1]),
        pltpu.make_async_copy(wkv_h.at[mine_z], kvw.at[(xh, y, c, m) + mine_z], lsem.at[2]),
        pltpu.make_async_copy(nbr_h, nbr, lsem.at[3]),
        pltpu.make_async_copy(cot_h, cot, lsem.at[4]),
        pltpu.make_async_copy(dec_h, dec, lsem.at[5]),
        pltpu.make_async_copy(bias_h, bias_raw, lsem.at[6]),
        pltpu.make_async_copy(wkv_h.at[lower], kvw.at[xh, y, c, m, lower], lsem.at[7]),
    ]
    for one in local_in:
        one.start()

    barrier = pltpu.get_barrier_semaphore()
    each(1, 16, lambda j: pl.semaphore_signal(barrier, inc=1, device_id=at_n(j), device_id_type=MESH))
    each(1, 8, lambda j: pl.semaphore_signal(barrier, inc=1, device_id=at_z(j), device_id_type=MESH))
    pl.semaphore_signal(barrier, inc=1, device_id=at_x(1), device_id_type=MESH)
    pl.semaphore_signal(barrier, inc=1, device_id=at_x(3), device_id_type=MESH)
    pl.semaphore_wait(barrier, 24)

    halves = [
        (qw, [(pl.ds(0, 16), every), (pl.ds(16, 16), every)]),
        (ow, [(every, pl.ds(0, 512)), (every, pl.ds(512, 512))]),
    ]

    def first(t, h, j, arriving):
        buf, parts = halves[t]
        sy, sx, sm = y, xh, m
        if arriving:
            if h == 0:
                sy = (y + 4 - j) % 4
            else:
                far = (x + 4 - j) % 4
                sx, sm = far // 2, far % 2
        ref = buf.at[(sx, sy, c, sm) + parts[h]]
        return remote(ref, ref, ag_s.at[t, 0, h, j], ag_r.at[t, 0, h, j], at_y(j) if h == 0 else at_x(j))

    def second(t, h, j, arriving):
        buf, parts = halves[t]
        if h == 0:
            far = (x + 4 - j) % 4 if arriving else x
            ref = buf.at[(far // 2, every, c, far % 2) + parts[h]]
        else:
            sy = (y + 4 - j) % 4 if arriving else y
            ref = buf.at[(every, sy, c, every) + parts[h]]
        return remote(ref, ref, ag_s.at[t, 1, h, j], ag_r.at[t, 1, h, j], at_x(j) if h == 0 else at_y(j))

    def third(t, arriving):
        buf = halves[t][0]
        ref = buf.at[:, :, (1 - c) if arriving else c]
        return remote(ref, ref, ag_s.at[t, 2, 0, 0], ag_r.at[t, 2, 0, 0], at_core)

    def block(h, a1, a2, lo, count):
        px, py = (a2, a1) if h == 0 else (a1, a2)
        return kvw.at[px // 2, py, c, px % 2, pl.ds(64 + 32 * h + lo, count)]

    parts_of = ((0, 32), (0, 32), (0, 16), (16, 16))
    here = ((y, x), (x, y))
    at_axis = ((at_y, at_x), (at_x, at_y))

    def move(h, axis, b, kind, arriving):
        step = 1 if kind % 2 == 0 else 3
        off = 0 if kind < 2 else 4 - step
        if arriving:
            off = (off + 4 - step) % 4
        m1, m2 = here[h]
        if axis == 0:
            ref = block(h, (m1 + off) % 4, m2, *parts_of[kind])
        else:
            ref = block(h, (m1 + b) % 4, (m2 + off) % 4, *parts_of[kind])
        return remote(
            ref, ref, kv_ss.at[h, axis, b, kind], kv_rs.at[h, axis, b, kind], at_axis[h][axis](step)
        )

    def across(h, e, arriving):
        cc = (1 - c) if arriving else c
        a2 = (here[h][1] + e) % 4
        rows = pl.ds(64 + 32 * h, 32)
        if h == 0:
            ref = kvw.at[a2 // 2, :, cc, a2 % 2, rows]
        else:
            ref = kvw.at[:, a2, cc, :, rows]
        return remote(ref, ref, kc_s.at[h, e], kc_r.at[h, e], at_core)

    def plane_first(j, arriving):
        sy = (y + 4 - j) % 4 if arriving else y
        ref = kvw.at[(xh, sy, c, m) + mine_z]
        return remote(ref, ref, c_ss.at[0, j], c_rs.at[0, j], at_y(j))

    def plane_second(j, arriving):
        far = (x + 4 - j) % 4 if arriving else x
        ref = kvw.at[(far // 2, every, c, far % 2) + mine_z]
        return remote(ref, ref, c_ss.at[1, j], c_rs.at[1, j], at_x(j))

    def ring(k, way, sub, arriving):
        off = k if arriving else k - 1
        place = (z + (8 - off if way == 0 else off)) % 8
        ref = kvw.at[(sub, every, c, every) + piece(place)]
        return remote(ref, ref, z_ss.at[k, way, sub], z_rs.at[k, way, sub], at_z(1 if way == 0 else 7))

    def across_z(off, arriving):
        cc = (1 - c) if arriving else c
        ref = kvw.at[(every, every, cc, every) + piece((z + off) % 8)]
        return remote(ref, ref, kz_s.at[off], kz_r.at[off], at_core)

    def ring_pass(k, sub):
        for way in range(2):
            ring(k, way, sub, True).wait_recv()
            if k < 3 or (k == 3 and sub == way):
                ring(k + 1, way, sub, False).start()

    def move_pair(h, axis, b, first_kind, arriving):
        for kind in (first_kind, first_kind + 1):
            one = move(h, axis, b, kind, arriving)
            one.wait_recv() if arriving else one.start()

    local_in[2].wait()
    each(1, 4, lambda j: plane_first(j, False).start())
    local_in[0].wait()
    for h in range(2):
        each(1, 4, lambda j, h=h: first(0, h, j, False).start())
    local_in[7].wait()
    for h in range(2):
        move_pair(h, 0, 0, 0, False)
        move_pair(h, 1, 0, 0, False)
    local_in[1].wait()
    for h in range(2):
        each(1, 4, lambda j, h=h: first(1, h, j, False).start())

    each(1, 4, lambda j: plane_first(j, True).wait_recv())
    each(1, 4, lambda j: plane_second(j, False).start())
    for h in range(2):
        each(1, 4, lambda j, h=h: first(0, h, j, True).wait_recv())
        each(1, 4, lambda j, h=h: second(0, h, j, False).start())
    for h in range(2):
        each(1, 4, lambda j, h=h: first(1, h, j, True).wait_recv())
        each(1, 4, lambda j, h=h: second(1, h, j, False).start())
    for h in range(2):
        move_pair(h, 0, 0, 0, True)
        move_pair(h, 0, 0, 2, False)
        move_pair(h, 1, 3, 0, False)
        move_pair(h, 1, 1, 0, False)
    each(1, 4, lambda j: plane_second(j, True).wait_recv())
    for sub in range(2):
        for way in range(2):
            ring(1, way, sub, False).start()
    across_z(0, False).start()
    for h in range(2):
        each(1, 4, lambda j, h=h: second(0, h, j, True).wait_recv())
    third(0, False).start()
    for h in range(2):
        move_pair(h, 1, 0, 0, True)
        move_pair(h, 1, 0, 2, False)
    local_in[3].wait()
    third(0, True).wait_recv()

    def query_block(i):
        r = pl.ds(pl.multiple_of(i * 128, 128), 128)
        found = dot_nn(nbr[r, :], qw[...].reshape(1024, 512)).astype(BF)
        queries[pl.ds(2 * i, 2)] = found.reshape(2, 64, 512)

    each(0, 4, query_block)

    def slot_of(t):
        found = 0
        for s in range(8):
            found = found + jnp.where(shift[s % 2, s // 2] == t, s, 0)
        return jnp.minimum(found, 7)

    def query_send(t):
        qs[t] = queries[slot_of(t)]
        remote(qs.at[t], qr.at[t], qx_s.at[t], qx_r.at[t], at_n(16 - t)).start()

    each(1, 16, query_send)
    qr[0] = queries[slot_of(0)]

    ring_pass(1, 0)
    for h in range(2):
        move_pair(h, 0, 0, 2, True)
        move_pair(h, 1, 2, 0, False)
        across(h, 0, False).start()
    ring_pass(1, 1)
    across_z(1, False).start()
    across_z(7, False).start()

    local_in[6].wait()
    for h in range(8):
        turned = bias_raw[h]
        rolled = pltpu.roll(turned, 64, 1)
        lane = lax.broadcasted_iota(jnp.int32, (64, 128), 1)
        keep = (lane < 64) == (m == 0)
        bias_t[h * 64 : (h + 1) * 64, :] = jnp.where(keep, turned, rolled)

    for h in range(2):
        each(1, 4, lambda j, h=h: second(1, h, j, True).wait_recv())
    third(1, False).start()
    for b in (3, 1):
        for h in range(2):
            move_pair(h, 1, b, 0, True)
            move_pair(h, 1, b, 2, False)
    ring_pass(2, 0)
    third(1, True).wait_recv()
    local_in[4].wait()

    def gmix_block(i):
        r = pl.ds(pl.multiple_of(i * 128, 128), 128)
        gmix[r, :] = dot_nt(cot[r, :], ow[...].reshape(512, 1024)).astype(BF)

    each(0, 4, gmix_block)

    ring_pass(2, 1)
    across_z(2, False).start()
    across_z(6, False).start()
    for h in range(2):
        move_pair(h, 1, 2, 0, True)
        move_pair(h, 1, 2, 2, False)
        across(h, 3, False).start()
        across(h, 1, False).start()
    nbr_t[...] = nbr[...].T
    ring_pass(3, 0)
    ring_pass(3, 1)
    across_z(3, False).start()
    across_z(5, False).start()
    for h in range(2):
        for b in (0, 3, 1, 2):
            move_pair(h, 1, b, 2, True)
        across(h, 2, False).start()
    for way in range(2):
        ring(4, way, way, True).wait_recv()
    across_z(4, False).start()
    local_in[5].wait()
    each(0, 8, lambda off: across_z(off, True).wait_recv())
    for h in range(2):
        each(0, 4, lambda e, h=h: across(h, e, True).wait_recv())

    gkv[...] = jnp.zeros_like(gkv)

    def kv_block(i):
        cols = pl.ds(pl.multiple_of(i * 512, 512), 512)
        gkv[...] += dot_nn(dec[:, cols], kvw[i // 4, i % 4].reshape(512, 1024))

    each(0, 8, kv_block)
    kv[...] = gkv[...].astype(BF)

    each(1, 16, lambda t: remote(qr.at[t], qr.at[t], qx_s.at[t], qx_r.at[t], at_n(t)).wait_recv())

    row_head = lax.broadcasted_iota(jnp.int32, (256, 256), 0) // 64
    col_head = lax.broadcasted_iota(jnp.int32, (256, 256), 1) // 64
    same = row_head == col_head

    def spread(block):
        return jnp.where(same, jnp.concatenate([block] * 4, axis=0), jnp.zeros((), BF))

    def gather_diag(full):
        kept = jnp.where(same, full, 0.0)
        return kept[0:64] + kept[64:128] + kept[128:192] + kept[192:256]

    def stretch(s, lo, hi, g):
        q_both = jnp.concatenate([qr[shift[0, s]], qr[shift[1, s]]], axis=0)
        rows_kv = pl.ds(pl.multiple_of(s * 64, 64), 64)
        rows_tok = pl.ds(pl.multiple_of(s * 128, 128), 128)
        keys = spread(kv[rows_kv, lo:hi])
        vals = spread(kv[rows_kv, 512 + lo : 512 + hi])
        q = q_both[:, lo:hi]
        gm = gmix[rows_tok, lo:hi]
        score = dot_nt(keys, q) * 0.125 + bias_t[lo:hi, :]
        grad_p = dot_nt(vals, gm)
        score = score.reshape(4, 64, 128)
        grad_p = grad_p.reshape(4, 64, 128)
        top = jnp.max(score, axis=1, keepdims=True)
        e = jnp.exp(score - top)
        w = e * (1.0 / jnp.sum(e, axis=1, keepdims=True))
        probs = w.astype(BF).reshape(256, 128)
        inner = jnp.sum(w * grad_p, axis=1, keepdims=True)
        gscore = (w * (grad_p - inner)).astype(BF).reshape(256, 128)
        mix[rows_tok, lo:hi] = dot_tn(probs, vals).astype(BF)
        gq = (dot_tn(gscore, keys) * 0.125).astype(BF)
        gq_loc[g, pl.ds(2 * s, 2)] = gq.reshape(2, 64, 256)
        gkv[rows_kv, lo:hi] = gather_diag(dot_nn(gscore, q)) * 0.125
        gkv[rows_kv, 512 + lo : 512 + hi] = gather_diag(dot_nn(probs, gm))

    gr = (gr_a, gr_b)

    def grad_copy(g, t):
        return remote(gs.at[g, t], gr[g].at[t], gx_s.at[g, t], gx_r.at[g, t], at_n(t))

    def grad_send(g, t):
        gs[g, t] = gq_loc[g, slot_of(t)]
        grad_copy(g, t).start()

    other_rows = pl.ds(pl.multiple_of((1 - m) * 128, 128), 128)

    def mp_copy(g):
        return remote(gkv_s.at[g], gkv_r.at[g], mp_s.at[g], mp_r.at[g], at_mp)

    for g in range(2):
        lo, hi = g * 256, (g + 1) * 256
        each(0, 4, lambda s, g=g, lo=lo, hi=hi: stretch(s, lo, hi, g))
        if g == 1:
            mix_t = mix[...].T
            for p in range(2):
                part = dot_nn(mix_t[p * 256 : (p + 1) * 256], cot[...])
                ored[p] = part.astype(BF).reshape(4, 2, 2, 16, 1024)
            o1 = remote(ored.at[:, :, 1 - c], or1, r1_s.at[0], r1_r.at[0], at_core)
            o1.start()

        each(1, 16, lambda t, g=g: grad_send(g, t))
        gr[g][0] = gq_loc[g, slot_of(0)]
        gkv_s[g, :, 0:256] = gkv[other_rows, lo:hi].astype(BF)
        gkv_s[g, :, 256:512] = gkv[other_rows, 512 + lo : 512 + hi].astype(BF)
        mp_copy(g).start()

    def att_block(i):
        r = pl.ds(pl.multiple_of(i * 128, 128), 128)
        att[r, :] = dot_nn(mix[r, :], ow[...].reshape(512, 1024)).astype(BF)

    each(0, 4, att_block)
    out_att = pltpu.make_async_copy(att, att_o, osem.at[0])
    out_att.start()

    o1.wait_recv()
    oa1[...] = (ored[:, :, c].astype(F32) + or1[...].astype(F32)).astype(BF)

    def o2(j):
        return remote(
            oa1.at[:, (y + j) % 4], or2.at[j], r2_s.at[0, j], r2_r.at[0, j], at_y(j)
        )

    each(1, 4, lambda j: o2(j).start())

    def grads_back(g):
        lo, hi = g * 256, (g + 1) * 256
        each(1, 16, lambda t: grad_copy(g, t).wait_recv())
        for s in range(8):
            gq_all[s * 64 : (s + 1) * 64, lo:hi] = gr[g][shift[s % 2, s // 2]]
        for p in range(2):
            part = dot_nn(nbr_t[p * 512 : (p + 1) * 512, :], gq_all[:, lo:hi])
            wred[g, p] = part.astype(BF).reshape(4, 2, 2, 32, 256)
        w1(g).start()

    def w1(g):
        return remote(wred.at[g, :, :, 1 - c], wr1.at[g], r1_s.at[1 + g], r1_r.at[1 + g], at_core)

    def core_sum(g):
        w1(g).wait_recv()
        wa1[g] = (wred[g, :, :, c].astype(F32) + wr1[g].astype(F32)).astype(BF)

    def w2(g, j):
        far = (x + j) % 4
        if g == 0:
            src, dst, device = wa1.at[0, :, (y + j) % 4], wr2y.at[j], at_y(j)
        else:
            src, dst, device = wa1.at[1, far // 2, :, far % 2], wr2x.at[j], at_x(j)
        return remote(src, dst, r2_s.at[1 + g, j], r2_r.at[1 + g, j], device)

    def w3(g, j):
        far = (x + j) % 4
        if g == 0:
            src, device = wa2y.at[far // 2, far % 2], at_x(j)
        else:
            src, device = wa2x.at[(y + j) % 4], at_y(j)
        return remote(src, wr3.at[g, j], r3_s.at[1 + g, j], r3_r.at[1 + g, j], device)

    grads_back(0)

    def o3(j):
        far = (x + j) % 4
        return remote(oa2.at[far // 2, far % 2], or3.at[j], r3_s.at[0, j], r3_r.at[0, j], at_x(j))

    core_sum(0)
    each(1, 4, lambda j: w2(0, j).start())
    grads_back(1)
    core_sum(1)
    each(1, 4, lambda j: w2(1, j).start())
    each(1, 4, lambda j: o2(j).wait_recv())
    oa2[...] = (
        oa1[:, y].astype(F32) + or2[1].astype(F32) + or2[2].astype(F32) + or2[3].astype(F32)
    ).astype(BF)

    each(1, 4, lambda j: o3(j).start())
    each(1, 4, lambda j: w2(0, j).wait_recv())
    wa2y[...] = (
        wa1[0, :, y].astype(F32) + wr2y[1].astype(F32) + wr2y[2].astype(F32) + wr2y[3].astype(F32)
    ).astype(BF)
    each(1, 4, lambda j: w3(0, j).start())

    def neigh_block(i):
        r = pl.ds(pl.multiple_of(i * 128, 128), 128)
        neigh[r, :] = dot_nt(gq_all[r, :], qw[...].reshape(1024, 512)).astype(BF)

    each(0, 4, neigh_block)
    out_neigh = pltpu.make_async_copy(neigh, neigh_o, osem.at[2])
    out_neigh.start()

    each(1, 4, lambda j: w2(1, j).wait_recv())
    wa2x[...] = (
        wa1[1, xh, :, m].astype(F32) + wr2x[1].astype(F32) + wr2x[2].astype(F32) + wr2x[3].astype(F32)
    ).astype(BF)
    each(1, 4, lambda j: w3(1, j).start())

    mine = pl.ds(pl.multiple_of(m * 128, 128), 128)
    for g in range(2):
        lo, hi = g * 256, (g + 1) * 256
        mp_copy(g).wait_recv()
        kv_sum[:, lo:hi] = (gkv[mine, lo:hi] + gkv_r[g, :, 0:256].astype(F32)).astype(BF)
        kv_sum[:, 512 + lo : 512 + hi] = (
            gkv[mine, 512 + lo : 512 + hi] + gkv_r[g, :, 256:512].astype(F32)
        ).astype(BF)

    def rows_block(i):
        cols = pl.ds(pl.multiple_of(i * 512, 512), 512)
        rows[:, cols] = dot_nt(kv_sum[...], kvw[i // 4, i % 4].reshape(512, 1024)).astype(BF)

    each(1, 4, lambda j: o3(j).wait_recv())
    o_sum = (
        oa2[xh, m].astype(F32) + or3[1].astype(F32) + or3[2].astype(F32) + or3[3].astype(F32)
    )
    each(0, 4, rows_block)
    for g in range(2):
        each(1, 4, lambda j, g=g: w3(g, j).wait_recv())
        own = wa2y[xh, m] if g == 0 else wa2x[y]
        w_sum = own.astype(F32) + wr3[g, 1].astype(F32) + wr3[g, 2].astype(F32) + wr3[g, 3].astype(F32)
        for p in range(4):
            zs[4 * g + p, 0:16] = w_sum[(p // 2) * 16 : (p // 2) * 16 + 16, (p % 2) * 128 : (p % 2) * 128 + 128].astype(BF)
    for p in range(8):
        zs[p, 16:32] = o_sum[:, p * 128 : (p + 1) * 128].astype(BF)

    def z1(j):
        return remote(zs.at[(z + j) % 8], zr.at[j], r4_s.at[j], r4_r.at[j], at_z(j))

    each(1, 8, lambda j: z1(j).start())
    each(4, 8, rows_block)
    out_rows = pltpu.make_async_copy(rows, rows_o, osem.at[1])
    out_rows.start()
    total = zs[z].astype(F32)
    each(1, 8, lambda j: z1(j).wait_recv())
    for j in range(1, 8):
        total = total + zr[j].astype(F32)
    za[...] = total.astype(BF)

    def z2(j, arriving):
        place = (z + 8 - j) % 8 if arriving else z
        return remote(za, zg.at[place], r5_s.at[j], r5_r.at[j], at_z(j))

    each(1, 8, lambda j: z2(j, False).start())
    zg[z] = za[...]
    each(1, 8, lambda j: z2(j, True).wait_recv())
    for p in range(8):
        top_row, left = ((p // 2) % 2) * 16, (p // 4) * 256 + (p % 2) * 128
        gqw_v[top_row : top_row + 16, left : left + 128] = zg[p, 0:16].astype(F32)
        gow_v[:, p * 128 : (p + 1) * 128] = zg[p, 16:32].astype(F32)
    out_q = pltpu.make_async_copy(gqw_v, gqw_o, osem.at[3])
    out_o = pltpu.make_async_copy(gow_v, gow_o, osem.at[4])
    out_q.start()
    out_o.start()

    for t in range(2):
        for h in range(2):
            each(1, 4, lambda j, t=t, h=h: first(t, h, j, False).wait_send())
            each(1, 4, lambda j, t=t, h=h: second(t, h, j, False).wait_send())
        third(t, False).wait_send()
    each(1, 4, lambda j: plane_first(j, False).wait_send())
    each(1, 4, lambda j: plane_second(j, False).wait_send())
    for h in range(2):
        for kind in range(4):
            move(h, 0, 0, kind, False).wait_send()
            each(0, 4, lambda b, h=h, kind=kind: move(h, 1, b, kind, False).wait_send())
        each(0, 4, lambda e, h=h: across(h, e, False).wait_send())
    for k in range(1, 5):
        for way in range(2):
            for sub in range(2):
                if k < 4 or sub == way:
                    ring(k, way, sub, False).wait_send()
    each(0, 8, lambda off: across_z(off, False).wait_send())
    each(1, 16, lambda t: remote(qs.at[t], qr.at[t], qx_s.at[t], qx_r.at[t], at_n(t)).wait_send())
    for g in range(2):
        each(1, 16, lambda t, g=g: grad_copy(g, t).wait_send())
        mp_copy(g).wait_send()
        w1(g).wait_send()
    o1.wait_send()
    each(1, 4, lambda j: o2(j).wait_send())
    each(1, 4, lambda j: o3(j).wait_send())
    for g in range(2):
        each(1, 4, lambda j, g=g: w2(g, j).wait_send())
        each(1, 4, lambda j, g=g: w3(g, j).wait_send())
    each(1, 8, lambda j: z1(j).wait_send())
    each(1, 8, lambda j: z2(j, False).wait_send())
    out_att.wait()
    out_rows.wait()
    out_neigh.wait()
    out_q.wait()
    out_o.wait()


def hand_over(*refs):
    held, sem = refs[10:15], refs[15]
    into = [pltpu.make_async_copy(refs[i], held[i], sem.at[0, i]) for i in range(5)]
    out = [pltpu.make_async_copy(held[i], refs[5 + i], sem.at[1, i]) for i in range(5)]
    for one in into:
        one.start()
    for one, after in zip(into, out):
        one.wait()
        after.start()
    for one in out:
        one.wait()


def local(dec_rows, owner_shift, nbr_rows, cot_attended, query_w, kv_w, out_w, pos_bias):
    vmem = pltpu.VMEM
    dma = pltpu.SemaphoreType.DMA
    anywhere = pl.BlockSpec(memory_space=pl.ANY)
    scratch = [
        vmem((2, 4, 2, 2, 32, 512), BF), vmem((2, 4, 2, 2, 128, 1024), BF), vmem((2, 4, 2, 2, 16, 1024), BF),
        vmem((256, 4096), BF), vmem((512, 1024), BF), vmem((1024, 512), BF), vmem((512, 1024), BF),
        vmem((8, 64, 128), F32), vmem((512, 128), F32),
        vmem((8, 64, 512), BF), vmem((16, 64, 512), BF), vmem((16, 64, 512), BF), vmem((256, 1024), BF),
        vmem((512, 512), BF), vmem((512, 512), BF), vmem((2, 8, 64, 256), BF),
        vmem((2, 16, 64, 256), BF), vmem((16, 64, 256), BF), vmem((16, 64, 256), BF), vmem((512, 512), BF),
        vmem((256, 1024), F32), vmem((2, 128, 512), BF), vmem((2, 128, 512), BF), vmem((128, 1024), BF),
        vmem((512, 1024), BF), vmem((128, 4096), BF), vmem((512, 1024), BF),
        vmem((2, 2, 4, 2, 2, 32, 256), BF), vmem((2, 4, 2, 2, 16, 1024), BF),
        vmem((2, 2, 4, 2, 32, 256), BF), vmem((2, 4, 2, 16, 1024), BF),
        vmem((2, 2, 4, 2, 32, 256), BF), vmem((2, 4, 2, 16, 1024), BF),
        vmem((4, 2, 2, 32, 256), BF), vmem((4, 4, 32, 256), BF), vmem((4, 2, 2, 16, 1024), BF),
        vmem((2, 2, 32, 256), BF), vmem((4, 32, 256), BF), vmem((2, 2, 16, 1024), BF),
        vmem((2, 4, 32, 256), BF), vmem((4, 16, 1024), BF),
        vmem((8, 32, 128), BF), vmem((8, 32, 128), BF), vmem((32, 128), BF), vmem((8, 32, 128), BF),
        vmem((32, 512), F32), vmem((16, 1024), F32),
        dma((8,)), dma((2, 3, 2, 4)), dma((2, 3, 2, 4)), dma((2, 2, 4, 4)), dma((2, 2, 4, 4)), dma((2, 4)), dma((2, 4)),
        dma((2, 4)), dma((2, 4)), dma((5, 2, 2)), dma((5, 2, 2)), dma((8,)), dma((8,)),
        dma((16,)), dma((16,)), dma((2, 16)), dma((2, 16)),
        dma((2,)), dma((2,)), dma((3,)), dma((3,)), dma((3, 4)), dma((3, 4)), dma((3, 4)), dma((3, 4)),
        dma((8,)), dma((8,)), dma((8,)), dma((8,)), dma((5,)),
    ]
    shapes = (
        jax.ShapeDtypeStruct((512, 1024), BF),
        jax.ShapeDtypeStruct((128, 4096), BF),
        jax.ShapeDtypeStruct((512, 1024), BF),
        jax.ShapeDtypeStruct((32, 512), F32),
        jax.ShapeDtypeStruct((16, 1024), F32),
    )
    results = pl.pallas_call(
        kernel,
        out_shape=shapes,
        in_specs=[pl.BlockSpec(memory_space=pltpu.SMEM)] + [anywhere] * 7,
        out_specs=[anywhere] * 5,
        scratch_shapes=scratch,
        compiler_params=pltpu.CompilerParams(
            collective_id=0, has_side_effects=True, vmem_limit_bytes=60 * 2**20
        ),
        cost_estimate=pl.CostEstimate(flops=7 * 10**9, bytes_accessed=12 * 2**20, transcendentals=2 * 10**6),
        name="retrieval",
    )(
        owner_shift[0].T,
        dec_rows[0],
        nbr_rows.reshape(512, 1024),
        cot_attended.reshape(512, 1024),
        query_w,
        kv_w,
        out_w,
        jnp.swapaxes(pos_bias, 1, 2),
    )
    attended, grad_rows, grad_neigh, grad_query_w, grad_out_w = pl.pallas_call(
        hand_over,
        out_shape=shapes,
        in_specs=[anywhere] * 5,
        out_specs=[anywhere] * 5,
        scratch_shapes=[vmem(one.shape, one.dtype) for one in shapes] + [dma((2, 5))],
        name="hand_over",
    )(*results)
    return (
        attended.reshape(1, 4, 2, 64, 1024),
        grad_rows[None],
        grad_neigh.reshape(1, 8, 64, 1024),
        grad_query_w,
        grad_out_w,
    )


def solution(mesh):
    placed = (
        P("dp", "nbr", None),
        P("dp", None, None),
        P("dp", "nbr", "mp", None),
        P("dp", "nbr", None, "mp", None),
        P(("nbr", "mp"), None),
        P(("nbr", "mp"), None),
        P(("nbr", "mp"), None),
        P(),
    )
    return jax.shard_map(
        local,
        mesh=mesh,
        in_specs=placed,
        out_specs=(
            P("dp", "nbr", None, "mp", None),
            P("dp", ("nbr", "mp"), None),
            P("dp", "nbr", "mp", None),
            P(("nbr", "mp"), None),
            P(("nbr", "mp"), None),
        ),
        check_vma=False,
    )
```

time: 120 us -> 106 us (0.88)
  the two profiles are of different devices: /device:TPU:2 before, /device:TPU:8 now
where the time goes in v2:
time: 106 us
  Pallas kernels  105 us (99%)
    pallas_call x1, Pallas kernels, local(): pl.pallas_call(kernel, out_shape=shapes, in_specs=[pl.BlockSpec(memory_sp...  102 us
    pallas_call x1, Pallas kernels, local(): pl.pallas_call(hand_over, out_shape=shapes, in_specs=[anywhere] * 5, out_...  3 us

profile of v2, /device:TPU:8, one launch (start us, length us, event | category | flops | bytes accessed | tf_op | source)
XLA Modules:
  0.0 105.6 jit_solution(1433443965521075616)
XLA Ops:
  0.6 102.0 %retrieval.1 = (bf16[512,1024]{1,0:T(8,128)(2,1)}, bf16[128,4096]{1,0:T(8,128)(2,1)}, bf16[512,1024]{1,0:T(8,128)(2,1)}, f32[32,512]{1,0:T(8,128)}, f32[16,1024]{1,0:T(8,128)}) custom-call(s32[2,4]{1,0:T(2,128)} %bitcast.17, bf16[256,4096]{1,0:T(8,128)(2,1)} %bitcast.10, bf16[512,1024]{1,0:T(8,128)(2,1)} %bitcast.11, bf16[512,1024]{1,0:T(8,128)(2,1)} %bitcast.12, ...), custom_call_target="tpu_custom_call" | custom-call | flops 7000000000 | bytes 12582912 | tf_op jit(solution)/shard_map/retrieval/pallas_call | solution.py:616
  102.6 3.0 %hand_over.1 = (bf16[512,1024]{1,0:T(8,128)(2,1)}, bf16[128,4096]{1,0:T(8,128)(2,1)}, bf16[512,1024]{1,0:T(8,128)(2,1)}, f32[32,512]{1,0:T(8,128)}, f32[16,1024]{1,0:T(8,128)}) custom-call(bf16[512,1024]{1,0:T(8,128)(2,1)} %get-tuple-element.15.refs_0_, bf16[128,4096]{1,0:T(8,128)(2,1)} %get-tuple-element.16.refs_1_, ...), custom_call_target="tpu_custom_call" | custom-call | tf_op jit(solution)/shard_map/hand_over/pallas_call | solution.py:637

commit v3 on v2

--- a/solution.py
+++ b/solution.py
@@ -27,7 +27,7 @@
     att_o, rows_o, neigh_o, gqw_o, gow_o,
     qw, kvw, ow, dec, nbr, nbr_t, cot, bias_raw, bias_t,
     queries, qs, qr, kv, gmix, mix, gq_loc, gs, gr_a, gr_b, gq_all,
-    gkv, gkv_s, gkv_r, kv_sum, att, rows, neigh,
+    kv_acc, gkv, gkv_s, gkv_r, kv_sum, att, rows, neigh,
     wred, ored, wr1, or1, wa1, oa1, wr2y, wr2x, or2, wa2y, wa2x, oa2, wr3, or3, zs, zr, za, zg, gqw_v, gow_v,
     lsem, ag_s, ag_r, kv_ss, kv_rs, kc_s, kc_r, c_ss, c_rs, z_ss, z_rs, kz_s, kz_r, qx_s, qx_r, gx_s, gx_r, mp_s, mp_r,
     r1_s, r1_r, r2_s, r2_r, r3_s, r3_r, r4_s, r4_r, r5_s, r5_r, osem,
@@ -307,14 +307,21 @@
     for h in range(2):
         each(0, 4, lambda e, h=h: across(h, e, True).wait_recv())
 
-    gkv[...] = jnp.zeros_like(gkv)
-
-    def kv_block(i):
-        cols = pl.ds(pl.multiple_of(i * 512, 512), 512)
-        gkv[...] += dot_nn(dec[:, cols], kvw[i // 4, i % 4].reshape(512, 1024))
-
-    each(0, 8, kv_block)
-    kv[...] = gkv[...].astype(BF)
+    def project(g):
+        bands = [pl.ds(g * 256, 256), pl.ds(512 + g * 256, 256)]
+
+        def kv_block(i):
+            left = dec[:, pl.ds(pl.multiple_of(i * 1024, 1024), 1024)]
+            for k, band in enumerate(bands):
+                right = kvw[i // 2, pl.ds(2 * (i % 2), 2), :, :, :, band].reshape(1024, 256)
+                kv_acc[:, k * 256 : (k + 1) * 256] += dot_nn(left, right)
+
+        kv_acc[...] = jnp.zeros_like(kv_acc)
+        each(0, 4, kv_block)
+        for k, band in enumerate(bands):
+            kv[:, band] = kv_acc[:, k * 256 : (k + 1) * 256].astype(BF)
+
+    project(0)
 
     each(1, 16, lambda t: remote(qr.at[t], qr.at[t], qx_s.at[t], qx_r.at[t], at_n(t)).wait_recv())
 
@@ -369,6 +376,8 @@
 
     for g in range(2):
         lo, hi = g * 256, (g + 1) * 256
+        if g == 1:
+            project(1)
         each(0, 4, lambda s, g=g, lo=lo, hi=hi: stretch(s, lo, hi, g))
         if g == 1:
             mix_t = mix[...].T
@@ -382,7 +391,9 @@
         gr[g][0] = gq_loc[g, slot_of(0)]
         gkv_s[g, :, 0:256] = gkv[other_rows, lo:hi].astype(BF)
         gkv_s[g, :, 256:512] = gkv[other_rows, 512 + lo : 512 + hi].astype(BF)
-        mp_copy(g).start()
+
+    mp_copy(0).start()
+    mp_copy(1).start()
 
     def att_block(i):
         r = pl.ds(pl.multiple_of(i * 128, 128), 128)
@@ -590,7 +601,7 @@
         vmem((8, 64, 512), BF), vmem((16, 64, 512), BF), vmem((16, 64, 512), BF), vmem((256, 1024), BF),
         vmem((512, 512), BF), vmem((512, 512), BF), vmem((2, 8, 64, 256), BF),
         vmem((2, 16, 64, 256), BF), vmem((16, 64, 256), BF), vmem((16, 64, 256), BF), vmem((512, 512), BF),
-        vmem((256, 1024), F32), vmem((2, 128, 512), BF), vmem((2, 128, 512), BF), vmem((128, 1024), BF),
+        vmem((256, 512), F32), vmem((256, 1024), F32), vmem((2, 128, 512), BF), vmem((2, 128, 512), BF), vmem((128, 1024), BF),
         vmem((512, 1024), BF), vmem((128, 4096), BF), vmem((512, 1024), BF),
         vmem((2, 2, 4, 2, 2, 32, 256), BF), vmem((2, 4, 2, 2, 16, 1024), BF),
         vmem((2, 2, 4, 2, 32, 256), BF), vmem((2, 4, 2, 16, 1024), BF),

time: 106 us -> 102 us (0.962)
  the two profiles are of different devices: /device:TPU:8 before, /device:TPU:2 now
where the time goes in v3:
time: 102 us
  Pallas kernels  101 us (99%)
    pallas_call x1, Pallas kernels, local(): pl.pallas_call(kernel, out_shape=shapes, in_specs=[pl.BlockSpec(memory_sp...  98.3 us
    pallas_call x1, Pallas kernels, local(): pl.pallas_call(hand_over, out_shape=shapes, in_specs=[anywhere] * 5, out_...  3 us

profile of v3, /device:TPU:2, one launch (start us, length us, event | category | flops | bytes accessed | tf_op | source)
XLA Modules:
  0.0 101.9 jit_solution(4832848850506063931)
XLA Ops:
  0.6 98.3 %retrieval.1 = (bf16[512,1024]{1,0:T(8,128)(2,1)}, bf16[128,4096]{1,0:T(8,128)(2,1)}, bf16[512,1024]{1,0:T(8,128)(2,1)}, f32[32,512]{1,0:T(8,128)}, f32[16,1024]{1,0:T(8,128)}) custom-call(s32[2,4]{1,0:T(2,128)} %bitcast.17, bf16[256,4096]{1,0:T(8,128)(2,1)} %bitcast.10, bf16[512,1024]{1,0:T(8,128)(2,1)} %bitcast.11, bf16[512,1024]{1,0:T(8,128)(2,1)} %bitcast.12, ...), custom_call_target="tpu_custom_call" | custom-call | flops 7000000000 | bytes 12582912 | tf_op jit(solution)/shard_map/retrieval/pallas_call | solution.py:627
  98.9 3.0 %hand_over.1 = (bf16[512,1024]{1,0:T(8,128)(2,1)}, bf16[128,4096]{1,0:T(8,128)(2,1)}, bf16[512,1024]{1,0:T(8,128)(2,1)}, f32[32,512]{1,0:T(8,128)}, f32[16,1024]{1,0:T(8,128)}) custom-call(bf16[512,1024]{1,0:T(8,128)(2,1)} %get-tuple-element.15.refs_0_, bf16[128,4096]{1,0:T(8,128)(2,1)} %get-tuple-element.16.refs_1_, ...), custom_call_target="tpu_custom_call" | custom-call | tf_op jit(solution)/shard_map/hand_over/pallas_call | solution.py:648

commit v4 on v3

--- a/solution.py
+++ b/solution.py
@@ -517,28 +517,6 @@
     each(4, 8, rows_block)
     out_rows = pltpu.make_async_copy(rows, rows_o, osem.at[1])
     out_rows.start()
-    total = zs[z].astype(F32)
-    each(1, 8, lambda j: z1(j).wait_recv())
-    for j in range(1, 8):
-        total = total + zr[j].astype(F32)
-    za[...] = total.astype(BF)
-
-    def z2(j, arriving):
-        place = (z + 8 - j) % 8 if arriving else z
-        return remote(za, zg.at[place], r5_s.at[j], r5_r.at[j], at_z(j))
-
-    each(1, 8, lambda j: z2(j, False).start())
-    zg[z] = za[...]
-    each(1, 8, lambda j: z2(j, True).wait_recv())
-    for p in range(8):
-        top_row, left = ((p // 2) % 2) * 16, (p // 4) * 256 + (p % 2) * 128
-        gqw_v[top_row : top_row + 16, left : left + 128] = zg[p, 0:16].astype(F32)
-        gow_v[:, p * 128 : (p + 1) * 128] = zg[p, 16:32].astype(F32)
-    out_q = pltpu.make_async_copy(gqw_v, gqw_o, osem.at[3])
-    out_o = pltpu.make_async_copy(gow_v, gow_o, osem.at[4])
-    out_q.start()
-    out_o.start()
-
     for t in range(2):
         for h in range(2):
             each(1, 4, lambda j, t=t, h=h: first(t, h, j, False).wait_send())
@@ -557,6 +535,18 @@
                 if k < 4 or sub == way:
                     ring(k, way, sub, False).wait_send()
     each(0, 8, lambda off: across_z(off, False).wait_send())
+    total = zs[z].astype(F32)
+    each(1, 8, lambda j: z1(j).wait_recv())
+    for j in range(1, 8):
+        total = total + zr[j].astype(F32)
+    za[...] = total.astype(BF)
+
+    def z2(j, arriving):
+        place = (z + 8 - j) % 8 if arriving else z
+        return remote(za, zg.at[place], r5_s.at[j], r5_r.at[j], at_z(j))
+
+    each(1, 8, lambda j: z2(j, False).start())
+    zg[z] = za[...]
     each(1, 16, lambda t: remote(qs.at[t], qr.at[t], qx_s.at[t], qx_r.at[t], at_n(t)).wait_send())
     for g in range(2):
         each(1, 16, lambda t, g=g: grad_copy(g, t).wait_send())
@@ -569,10 +559,20 @@
         each(1, 4, lambda j, g=g: w2(g, j).wait_send())
         each(1, 4, lambda j, g=g: w3(g, j).wait_send())
     each(1, 8, lambda j: z1(j).wait_send())
-    each(1, 8, lambda j: z2(j, False).wait_send())
     out_att.wait()
     out_rows.wait()
     out_neigh.wait()
+    each(1, 8, lambda j: z2(j, True).wait_recv())
+    for p in range(8):
+        top_row, left = ((p // 2) % 2) * 16, (p // 4) * 256 + (p % 2) * 128
+        gqw_v[top_row : top_row + 16, left : left + 128] = zg[p, 0:16].astype(F32)
+        gow_v[:, p * 128 : (p + 1) * 128] = zg[p, 16:32].astype(F32)
+    out_q = pltpu.make_async_copy(gqw_v, gqw_o, osem.at[3])
+    out_o = pltpu.make_async_copy(gow_v, gow_o, osem.at[4])
+    out_q.start()
+    out_o.start()
+
+    each(1, 8, lambda j: z2(j, False).wait_send())
     out_q.wait()
     out_o.wait()
 

time: 102 us -> 102 us (level)
  no operation moved by 1% of the time
where the time goes in v4:
time: 102 us
  Pallas kernels  101 us (99%)
    pallas_call x1, Pallas kernels, local(): pl.pallas_call(kernel, out_shape=shapes, in_specs=[pl.BlockSpec(memory_sp...  97.9 us
    pallas_call x1, Pallas kernels, local(): pl.pallas_call(hand_over, out_shape=shapes, in_specs=[anywhere] * 5, out_...  3 us

profile of v4, /device:TPU:2, one launch (start us, length us, event | category | flops | bytes accessed | tf_op | source)
XLA Modules:
  0.0 101.5 jit_solution(8467128767545789460)
XLA Ops:
  0.6 97.9 %retrieval.1 = (bf16[512,1024]{1,0:T(8,128)(2,1)}, bf16[128,4096]{1,0:T(8,128)(2,1)}, bf16[512,1024]{1,0:T(8,128)(2,1)}, f32[32,512]{1,0:T(8,128)}, f32[16,1024]{1,0:T(8,128)}) custom-call(s32[2,4]{1,0:T(2,128)} %bitcast.17, bf16[256,4096]{1,0:T(8,128)(2,1)} %bitcast.10, bf16[512,1024]{1,0:T(8,128)(2,1)} %bitcast.11, bf16[512,1024]{1,0:T(8,128)(2,1)} %bitcast.12, ...), custom_call_target="tpu_custom_call" | custom-call | flops 7000000000 | bytes 12582912 | tf_op jit(solution)/shard_map/retrieval/pallas_call | solution.py:627
  98.5 3.0 %hand_over.1 = (bf16[512,1024]{1,0:T(8,128)(2,1)}, bf16[128,4096]{1,0:T(8,128)(2,1)}, bf16[512,1024]{1,0:T(8,128)(2,1)}, f32[32,512]{1,0:T(8,128)}, f32[16,1024]{1,0:T(8,128)}) custom-call(bf16[512,1024]{1,0:T(8,128)(2,1)} %get-tuple-element.15.refs_0_, bf16[128,4096]{1,0:T(8,128)(2,1)} %get-tuple-element.16.refs_1_, ...), custom_call_target="tpu_custom_call" | custom-call | tf_op jit(solution)/shard_map/hand_over/pallas_call | solution.py:648
